TPU v7x, 512 devices: a whole 4x8x8 slice. The times are simulated.
512 devices in a mesh: role: 2 (over core), ep: 128 (over z, x_lo, y), tp: 2 (over x_hi).
Axes of the slice: x: 4 (x_hi: 2, x_lo: 2; x = x_hi * 2 + x_lo), y: 8, z: 8, core: 2. Of those that a mesh axis runs over, the one named last changes fastest.
Arguments:
- pool_rows: bfloat16 [2, 1024, 7168], P('role', 'ep'), may hold values from -6 to 6
- kv_weight: bfloat16 [7168, 576], P('ep', ('role', 'tp')), may hold values from -0.0625 to 0.0625
- kv_gain: float32 [512], replicated, may hold values from 0.5 to 1.5
- latent_cache: bfloat16 [1024, 48, 576], P('ep'), may hold values from -4 to 4
- queries: bfloat16 [1024, 128, 576], P('ep', ('role', 'tp')), may hold values from -28 to 28
- cache_lengths: int32 [1024], P('ep'), may hold values from 2 to 48
- partner: int32 [128], replicated, may hold values from 0 to 127, each once
- expert_ids: int32 [1024, 8], P('ep'), may hold values from 0 to 15, all different within a row; in each aligned block of 8 rows (0 to 7, 8 to 15, ...) at most 8 rows name the same one
- expert_weights: float32 [1024, 8], P('ep'), may hold values from 0.05 to 0.5
- moe_gain: float32 [7168], replicated, may hold values from 0.5 to 1.5
- gate_up: bfloat16 [128, 7168, 512], P('ep', ('role', 'tp')), may hold values from -0.0625 to 0.0625
- down_proj: bfloat16 [128, 256, 7168], P('ep', None, ('role', 'tp')), may hold values from -0.125 to 0.125
Outputs:
- attention_out: bfloat16 [1024, 128, 512], P('ep', ('role', 'tp'))
- moe_out: bfloat16 [1024, 7168], P('ep', ('role', 'tp'))
Inputs may be any that keep to these rules, and one draw needn't show every extreme that they name: `expert_ids`: in each aligned block of 8 rows (the rows of one decode index) no expert is named by more than 8 rows; each row names 8 different experts. `partner`: A permutation of the decode indices.
All inputs are finite; a program needn't handle non-finite values.
Results may differ from a plain program's by a relative error of at most 0.0075.
Values may be sent and summed in bfloat16 or wider, within the bound.
A program may use at most 64 MiB of HBM per device.

v0:
```python
import jax
import jax.numpy as jnp
from jax import lax
from jax.sharding import PartitionSpec as P

LATENT = 512
ROPE = 64
NOPE = 128
FLIGHT = 16


EPSILON = 1e-06


def make_keys(raw_rows, positions, kv_gain):
    as_float = raw_rows.astype(jnp.float32)
    latent_part = as_float[:, :LATENT]
    inverse_rms = lax.rsqrt(jnp.mean(latent_part * latent_part, axis=1, keepdims=True) + EPSILON)
    latent_part = latent_part * inverse_rms * kv_gain[None, :]
    rotary_part = as_float[:, LATENT:].reshape(-1, ROPE // 2, 2)
    frequency = 10000.0 ** (-2.0 * jnp.arange(ROPE // 2, dtype=jnp.float32) / ROPE)
    angle_table = positions.astype(jnp.float32)[:, None] * frequency[None, :]
    cosine = jnp.cos(angle_table)
    sine_table = jnp.sin(angle_table)
    even_part = rotary_part[:, :, 0]
    odd_part = rotary_part[:, :, 1]
    rotated = jnp.stack(
        [even_part * cosine - odd_part * sine_table, even_part * sine_table + odd_part * cosine],
        axis=2,
    )
    return jnp.concatenate([latent_part, rotated.reshape(-1, ROPE)], axis=1).astype(jnp.bfloat16)


def attend(query_rows, cache_rows, length, prompt_key, new_key):
    score_scale = (NOPE + ROPE) ** (-0.5)
    row_count = query_rows.shape[0]
    cache_scores = (
        jnp.einsum("rhk,rlk->rhl", query_rows, cache_rows, preferred_element_type=jnp.float32)
        * score_scale
    )
    valid_mask = jnp.arange(cache_rows.shape[1], dtype=jnp.int32)[None, :] < length[:, None]
    cache_scores = jnp.where(valid_mask[:, None, :], cache_scores, -jnp.inf)
    prompt_scores = (
        jnp.einsum("rhk,ck->rhc", query_rows, prompt_key, preferred_element_type=jnp.float32)
        * score_scale
    )
    leading = jnp.arange(row_count, dtype=jnp.int32) == 0
    prompt_scores = jnp.where(leading[:, None, None], prompt_scores, -jnp.inf)
    own_scores = (
        jnp.einsum("rhk,rk->rh", query_rows, new_key, preferred_element_type=jnp.float32)
        * score_scale
    )
    row_top = jnp.maximum(
        jnp.maximum(jnp.max(cache_scores, axis=2), jnp.max(prompt_scores, axis=2)), own_scores
    )
    cache_exp = jnp.exp(cache_scores - row_top[:, :, None])
    prompt_exp = jnp.exp(prompt_scores - row_top[:, :, None])
    own_exp = jnp.exp(own_scores - row_top)
    denominator = jnp.sum(cache_exp, axis=2) + jnp.sum(prompt_exp, axis=2) + own_exp
    cache_weight = (cache_exp / denominator[:, :, None]).astype(jnp.bfloat16)
    prompt_weight = (prompt_exp / denominator[:, :, None]).astype(jnp.bfloat16)
    own_weight = (own_exp / denominator).astype(jnp.bfloat16)
    result = jnp.einsum(
        "rhl,rld->rhd", cache_weight, cache_rows[:, :, :LATENT], preferred_element_type=jnp.float32
    )
    result = result + jnp.einsum(
        "rhc,cd->rhd", prompt_weight, prompt_key[:, :LATENT], preferred_element_type=jnp.float32
    )
    result = result + own_weight.astype(jnp.float32)[:, :, None] * new_key[:, None, :LATENT].astype(
        jnp.float32
    )
    return result.astype(jnp.bfloat16)


def per_device(
    pool_rows,
    kv_weight,
    kv_gain,
    latent_cache,
    queries,
    cache_lengths,
    partner,
    expert_ids,
    expert_weights,
    moe_gain,
    gate_up,
    down_proj,
):
    row_count = latent_cache.shape[0]
    model_width = pool_rows.shape[2]
    pool_tokens = lax.all_gather(pool_rows, "role", axis=0, tiled=True)
    flat_tokens = pool_tokens.reshape(2 * row_count, model_width)
    latent_share = jnp.dot(
        flat_tokens,
        lax.all_gather(kv_weight, "ep", axis=0, tiled=True),
        preferred_element_type=jnp.float32,
    )
    raw_latent = lax.all_gather(
        latent_share.astype(jnp.bfloat16), ("role", "tp"), axis=1, tiled=True
    )
    prompt_raw = raw_latent[:row_count]
    new_raw = raw_latent[row_count:]
    ep_count = lax.axis_size("ep")
    ep_position = lax.axis_index("ep")
    ep_names = jnp.arange(ep_count, dtype=jnp.int32)
    every_block = lax.all_gather(prompt_raw, "ep", axis=0, tiled=True)
    source_index = jnp.sum(jnp.where(partner == ep_position, ep_names, 0))
    arrived_raw = lax.dynamic_slice_in_dim(every_block, source_index * row_count, row_count, 0)
    leading = (jnp.arange(row_count, dtype=jnp.int32) == 0).astype(jnp.int32)
    new_keys = make_keys(new_raw, cache_lengths + row_count * leading, kv_gain)
    prompt_keys = make_keys(
        arrived_raw, cache_lengths[0] + jnp.arange(row_count, dtype=jnp.int32), kv_gain
    )
    attention_out = attend(queries, latent_cache, cache_lengths, prompt_keys, new_keys)
    group_count = lax.axis_size(("role", "tp"))
    group_position = lax.axis_index(("role", "tp"))
    share_width = model_width // group_count
    decode_tokens = pool_tokens[1].astype(jnp.float32)
    scaled_tokens = (
        decode_tokens
        * lax.rsqrt(jnp.mean(decode_tokens * decode_tokens, axis=1, keepdims=True) + EPSILON)
        * moe_gain[None, :]
    )
    moe_share = lax.dynamic_slice_in_dim(
        scaled_tokens, group_position * share_width, share_width, 1
    ).astype(jnp.bfloat16)
    expert_count = min(ep_count, FLIGHT)
    split_count = ep_count // expert_count
    topk_count = expert_ids.shape[1]
    capacity = min(row_count, max(2, 2 * row_count * topk_count // expert_count))
    expert_names = jnp.arange(expert_count, dtype=jnp.int32)
    matches = expert_ids[:, :, None] == expert_names[None, None, :]
    routed = jnp.any(matches, axis=1).astype(jnp.int32)
    row_weight = jnp.sum(jnp.where(matches, expert_weights[:, :, None], 0.0), axis=1)
    slot_rank = jnp.cumsum(routed, axis=0) - routed
    slot_names = jnp.arange(capacity, dtype=jnp.int32)
    selection = routed.T[:, None, :] * (
        slot_rank.T[:, None, :] == slot_names[None, :, None]
    ).astype(jnp.int32)
    selection_float = selection.astype(jnp.float32)
    outgoing = jnp.einsum(
        "ecr,rd->ecd",
        selection_float.astype(jnp.bfloat16),
        moe_share,
        preferred_element_type=jnp.float32,
    ).astype(jnp.bfloat16)
    outgoing = jnp.repeat(outgoing, split_count, axis=0)
    combine_table = jnp.repeat(
        (selection_float * row_weight.T[:, None, :]).astype(jnp.bfloat16), split_count, axis=0
    )
    unit_width = gate_up.shape[2] // 2
    slot_block = lax.all_to_all(outgoing, "ep", split_axis=0, concat_axis=0, tiled=True)
    flat_rows = slot_block.reshape(-1, share_width)
    projected = jnp.dot(flat_rows, gate_up[0], preferred_element_type=jnp.float32)
    summed = lax.psum(projected, ("role", "tp"))
    hidden_units = (jax.nn.silu(summed[:, :unit_width]) * summed[:, unit_width:]).astype(
        jnp.bfloat16
    )
    partial_out = jnp.dot(hidden_units, down_proj[0], preferred_element_type=jnp.float32).astype(
        jnp.bfloat16
    )
    partial_out = partial_out.reshape(slot_block.shape[0], slot_block.shape[1], share_width)
    returned = lax.all_to_all(partial_out, "ep", split_axis=0, concat_axis=0, tiled=True)
    mixed_rows = jnp.einsum(
        "ecr,ecd->rd", combine_table, returned, preferred_element_type=jnp.float32
    )
    moe_out = mixed_rows.astype(jnp.bfloat16)
    return (attention_out, moe_out)


def solution(mesh):
    in_specs = (
        P("role", "ep", None),
        P("ep", ("role", "tp")),
        P(),
        P("ep", None, None),
        P("ep", ("role", "tp"), None),
        P("ep"),
        P(),
        P("ep", None),
        P("ep", None),
        P(),
        P("ep", ("role", "tp"), None),
        P("ep", None, ("role", "tp")),
    )
    out_specs = (P("ep", ("role", "tp"), None), P("ep", ("role", "tp")))
    return jax.shard_map(
        per_device, mesh=mesh, in_specs=in_specs, out_specs=out_specs, check_vma=False
    )
```

profile of v0, /device:TPU:4, one launch (start us, length us, event | category | flops | bytes accessed | tf_op | source)
XLA Modules:
  0.0 1336.6 jit_solution(9004442392484502992)
XLA Ops:
  8.0 0.0 copy-start
  8.0 0.0 all-reduce.2.cloned.1.call-start
  8.1 2.3 all_gather.12
  10.4 0.2 multiply_reduce_fusion
  10.6 0.8 fusion.34
  11.4 0.1 copy.57
  11.5 0.1 copy.58
  11.6 0.8 dynamic-slice
  12.3 0.3 convolution_convert_fusion.1
  12.7 0.2 broadcast_in_dim.52
  12.9 105.4 %all_to_all.10 = bf16[128,8,1792]{2,1,0:T(8,128)(2,1)S(1)} all-to-all(bf16[128,8,1792]{2,1,0:T(8,128)(2,1)S(1)} %bitcast.73), channel_id=1, replica_groups=mesh['role'=2,'ep'=128,'tp'=2] {'ep'}, dimensions={0} | all-to-all | bytes 7340032 | tf_op jit(solution)/shard_map/all_to_all | solution.py:152
  118.3 3.4 fusion
  121.7 0.0 all-reduce.2.cloned.1.call-update
  121.8 0.0 all-gather.4.cloned.1.call-start
  121.8 0.5 all-gather.4.cloned.1.call-update
  122.4 97.4 %all-reduce.2.cloned.1.call-done = f32[1024,512]{1,0:T(8,128)} async-done(((f32[1024,512]{1,0:T(8,128)}), f32[1024,512]{1,0:T(8,128)}) %all-reduce.2.cloned.1.call-update) | async-done | bytes 2097168 | tf_op jit(solution)/shard_map/psum | solution.py:155
  219.7 4.9 fusion.4
  224.6 14.8 %all-to-all-start.1 = ((bf16[128,8,1792]{2,1,0:T(8,128)(2,1)}), bf16[128,8,1792]{2,1,0:T(8,128)(2,1)}, u32[]{:S(2)}, u32[]{:S(2)}) async-start(bf16[128,8,1792]{2,1,0:T(8,128)(2,1)} %fusion.4), calls=%async_computation.1 | async-start | bytes 7340032 | tf_op jit(solution)/shard_map/all_to_all | solution.py:163
  239.4 0.0 copy-start.6
  239.4 0.0 copy-start.3
  239.4 0.0 copy-start.4
  239.4 0.0 copy-start.7
  239.4 0.0 copy-start.1
  239.4 0.0 copy-start.2
  239.4 0.0 copy-start.5
  239.4 0.0 all-gather.6.cloned.1.call-start
  239.5 488.2 %all-gather.4.cloned.1.call-done = bf16[7168,144]{1,0:T(8,128)(2,1)} async-done(((bf16[56,144]{1,0:T(8,128)(2,1)}), bf16[7168,144]{1,0:T(8,128)(2,1)}) %all-gather.4.cloned.1.call-update) | async-done | bytes 2064400 | tf_op jit(solution)/shard_map/all_gather | solution.py:95
  727.7 2.6 fusion.17
  730.4 12.6 all-gather
  742.9 0.1 reshape.291
  743.0 0.6 slice_convert_fusion
  743.6 0.0 all-gather.6.cloned.1.call-update
  743.7 0.6 fusion.64
  745.0 0.1 select_reduce_fusion
  745.1 0.1 copy.59
  745.2 0.1 copy.60
  745.3 0.2 broadcast_in_dim.51
  745.5 0.2 reshape.285
  745.8 0.0 copy-done.7
  745.8 0.1 iota_compare_fusion.2
  745.9 0.3 fusion.72
  746.3 0.1 copy.52
  746.4 0.1 copy.67
  746.5 0.1 copy.66
  746.5 0.1 multiply_reduce_fusion.1
  746.7 575.3 %all-gather.6.cloned.1.call-done = bf16[1024,576]{1,0:T(8,128)(2,1)} async-done(((bf16[8,576]{1,0:T(8,128)(2,1)}), bf16[1024,576]{1,0:T(8,128)(2,1)}) %all-gather.6.cloned.1.call-update) | async-done | bytes 1179664 | tf_op jit(solution)/shard_map/all_gather | solution.py:106
  1322.0 0.7 dynamic-slice_convert_fusion
  1322.7 0.1 copy.47
  1322.8 0.1 copy.65
  1322.8 0.1 copy.64
  1322.9 0.1 fusion.56
  1323.1 0.1 copy.50
  1323.2 0.1 copy.51
  1323.2 0.1 copy.55
  1323.3 0.1 copy.56
  1323.4 0.1 multiply_reduce_fusion.2
  1323.5 0.1 fusion.68
  1323.6 0.2 fusion.40
  1323.8 0.4 fusion.73
  1324.3 0.2 fusion.25
  1324.5 0.3 fusion.22
  1324.8 1.0 fusion.13
  1325.8 0.0 all-to-all-done.1
  1325.8 3.4 fusion.8
  (29 shorter events, 0.3 us)
Async XLA Ops:
  8.0 110.3 %copy-start = (bf16[1,1792,512]{2,1,0:T(8,128)(2,1)S(1)}, bf16[1,1792,512]{2,1,0:T(8,128)(2,1)}, u32[]{:S(2)}) copy-start(bf16[1,1792,512]{2,1,0:T(8,128)(2,1)} %param.22) | copy-start | bytes 5505028
  8.0 211.7 %all-reduce.2.cloned.1.call-start = ((), (), s32[]{:S(2)}) async-start(), calls=%async_computation.4 | async-start | bytes 4194304 | tf_op jit(solution)/shard_map/psum | solution.py:155
  121.8 606.0 %all-gather.4.cloned.1.call-start = ((), (), s32[]{:S(2)}) async-start(), calls=%async_computation.2 | async-start | bytes 3698688 | tf_op jit(solution)/shard_map/all_gather | solution.py:95
  224.6 1101.2 %all-to-all-start.1 = ((bf16[128,8,1792]{2,1,0:T(8,128)(2,1)}), bf16[128,8,1792]{2,1,0:T(8,128)(2,1)}, u32[]{:S(2)}, u32[]{:S(2)}) async-start(bf16[128,8,1792]{2,1,0:T(8,128)(2,1)} %fusion.4), calls=%async_computation.1 | async-start | bytes 7340032 | tf_op jit(solution)/shard_map/all_to_all | solution.py:163
  239.4 504.3 %copy-start.6 = (s32[128]{0:T(128)S(1)}, s32[128]{0:T(128)}, u32[]{:S(2)}) copy-start(s32[128]{0:T(128)} %param.18) | copy-start | bytes 1540
  239.4 505.6 %copy-start.3 = (s32[8,8]{1,0:T(8,128)S(1)}, s32[8,8]{1,0:T(8,128)}, u32[]{:S(2)}) copy-start(s32[8,8]{1,0:T(8,128)} %param.19) | copy-start | bytes 772
  239.4 505.6 %copy-start.4 = (f32[8,8]{1,0:T(8,128)S(1)}, f32[8,8]{1,0:T(8,128)}, u32[]{:S(2)}) copy-start(f32[8,8]{1,0:T(8,128)} %param.20) | copy-start | bytes 772
  239.4 506.4 %copy-start.7 = (s32[8]{0:T(128)S(1)}, s32[8]{0:T(128)}, u32[]{:S(2)}) copy-start(s32[8]{0:T(128)} %param.17) | copy-start | bytes 100
  239.4 506.5 %copy-start.1 = (bf16[8,48,576]{2,1,0:T(8,128)(2,1)S(1)}, bf16[8,48,576]{2,1,0:T(8,128)(2,1)}, u32[]{:S(2)}) copy-start(bf16[8,48,576]{2,1,0:T(8,128)(2,1)} %param.15) | copy-start | bytes 1327108
  239.4 506.5 %copy-start.2 = (bf16[8,32,576]{2,1,0:T(8,128)(2,1)S(1)}, bf16[8,32,576]{2,1,0:T(8,128)(2,1)}, u32[]{:S(2)}) copy-start(bf16[8,32,576]{2,1,0:T(8,128)(2,1)} %param.16) | copy-start | bytes 884740
  239.4 1084.1 %copy-start.5 = (f32[512]{0:T(512)S(1)}, f32[512]{0:T(512)}, u32[]{:S(2)}) copy-start(f32[512]{0:T(512)} %param.14) | copy-start | bytes 6148
  239.4 1082.5 %all-gather.6.cloned.1.call-start = ((), (), s32[]{:S(2)}) async-start(), calls=%async_computation.3 | async-start | bytes 1320960 | tf_op jit(solution)/shard_map/all_gather | solution.py:106
Sparse Core Ops, SparseCore 0:
  121.9 97.7 all-reduce.1
Sparse Core Ops, SparseCore 1:
  124.3 603.3 all-gather.3
  743.8 578.1 all-gather.5
where the time goes:
time: 1340 us
  waiting for transfers between devices  1160 us (87%)
  blocking collectives  120 us (9%)
  matrix products  16.8 us (1%)
  between operations  16.4 us (1%)
  starting transfers between devices  14.9 us (1%)
    all_gather x1, waiting for transfers between devices, per_device(): every_block = lax.all_gather(prompt_raw, 'ep', axis=0, tiled=True)  575 us
    all_gather x1, waiting for transfers between devices, per_device(): lax.all_gather(kv_weight, 'ep', axis=0, tiled=True)  488 us
    all_to_all x1, blocking collectives, per_device(): lax.all_to_all(outgoing, 'ep', split_axis=0, concat_axis=0, tiled=True)  105 us
    psum x1, waiting for transfers between devices, per_device(): summed = lax.psum(projected, ('role', 'tp'))  97.4 us
  transfers between devices with their start and end apart: 4, of which 3 were waited for; matrix products, arithmetic and copies ran while one was open for 1% of the time, Pallas kernels for 0%

commit v1 on v0

v1 whole, which is shorter than its diff:
```python
import functools

import jax
import jax.numpy as jnp
from jax import lax
from jax.experimental import pallas as pl
from jax.experimental.pallas import tpu as pltpu
from jax.sharding import PartitionSpec as P

MESH = pl.DeviceIdType.MESH
BF = jnp.bfloat16
F32 = jnp.float32
LATENT = 512
ROPE = 64
NOPE = 128
NX = 2
EPSILON = 1e-06


def make_keys(raw_rows, positions, kv_gain):
    as_float = raw_rows.astype(jnp.float32)
    latent_part = as_float[:, :LATENT]
    inverse_rms = lax.rsqrt(jnp.mean(latent_part * latent_part, axis=1, keepdims=True) + EPSILON)
    latent_part = latent_part * inverse_rms * kv_gain[None, :]
    rotary_part = as_float[:, LATENT:].reshape(-1, ROPE // 2, 2)
    frequency = 10000.0 ** (-2.0 * jnp.arange(ROPE // 2, dtype=jnp.float32) / ROPE)
    angle_table = positions.astype(jnp.float32)[:, None] * frequency[None, :]
    cosine = jnp.cos(angle_table)
    sine_table = jnp.sin(angle_table)
    even_part = rotary_part[:, :, 0]
    odd_part = rotary_part[:, :, 1]
    rotated = jnp.stack(
        [even_part * cosine - odd_part * sine_table, even_part * sine_table + odd_part * cosine],
        axis=2,
    )
    return jnp.concatenate([latent_part, rotated.reshape(-1, ROPE)], axis=1).astype(jnp.bfloat16)


def attend(query_rows, cache_rows, length, prompt_key, new_key):
    score_scale = (NOPE + ROPE) ** (-0.5)
    row_count = query_rows.shape[0]
    cache_scores = (
        jnp.einsum("rhk,rlk->rhl", query_rows, cache_rows, preferred_element_type=jnp.float32)
        * score_scale
    )
    valid_mask = jnp.arange(cache_rows.shape[1], dtype=jnp.int32)[None, :] < length[:, None]
    cache_scores = jnp.where(valid_mask[:, None, :], cache_scores, -jnp.inf)
    prompt_scores = (
        jnp.einsum("rhk,ck->rhc", query_rows, prompt_key, preferred_element_type=jnp.float32)
        * score_scale
    )
    leading = jnp.arange(row_count, dtype=jnp.int32) == 0
    prompt_scores = jnp.where(leading[:, None, None], prompt_scores, -jnp.inf)
    own_scores = (
        jnp.einsum("rhk,rk->rh", query_rows, new_key, preferred_element_type=jnp.float32)
        * score_scale
    )
    row_top = jnp.maximum(
        jnp.maximum(jnp.max(cache_scores, axis=2), jnp.max(prompt_scores, axis=2)), own_scores
    )
    cache_exp = jnp.exp(cache_scores - row_top[:, :, None])
    prompt_exp = jnp.exp(prompt_scores - row_top[:, :, None])
    own_exp = jnp.exp(own_scores - row_top)
    denominator = jnp.sum(cache_exp, axis=2) + jnp.sum(prompt_exp, axis=2) + own_exp
    cache_weight = (cache_exp / denominator[:, :, None]).astype(jnp.bfloat16)
    prompt_weight = (prompt_exp / denominator[:, :, None]).astype(jnp.bfloat16)
    own_weight = (own_exp / denominator).astype(jnp.bfloat16)
    result = jnp.einsum(
        "rhl,rld->rhd", cache_weight, cache_rows[:, :, :LATENT], preferred_element_type=jnp.float32
    )
    result = result + jnp.einsum(
        "rhc,cd->rhd", prompt_weight, prompt_key[:, :LATENT], preferred_element_type=jnp.float32
    )
    result = result + own_weight.astype(jnp.float32)[:, :, None] * new_key[:, None, :LATENT].astype(
        jnp.float32
    )
    return result.astype(jnp.bfloat16)


def fused_kernel(
    n, tok, gain, ids, wts, gu, dn, kvw, sel, asrc,
    moe_out, new_out, prompt_out,
    xsend, xpair, xg, pf, ps, pr, hb, out, cr, fs, cf,
    ts, tr, wb, pk, pkr, rn, ry, rzs, rz, rp,
    a0r, a1r, a2r, b1r, b2r, c2r, k5n, k7r, one, snd,
):
    role, ep, tp = lax.axis_index("role"), lax.axis_index("ep"), lax.axis_index("tp")
    z, x, y = ep // (NX * n), (ep // n) % NX, ep % n
    a_me = ep // n
    na = NX * n
    half = n // 2
    ch = n // 2
    ds = gu.shape[0]
    fe, kc = kvw.shape
    fa = n * fe
    group = role * 2 + tp

    def dev(r, zz, xx, yy, t):
        return (r, (zz * NX + xx) * n + yy, t)

    def slot(s, h, d):
        if s == 0:
            return h
        if s == half:
            return 2 + (half - 1) * 4 + h
        return 2 + (s - 1) * 4 + 2 * h + d

    n_sets = 2 + (half - 1) * 4 + 2

    def rcopy(src, dst, s, r, device):
        return pltpu.make_async_remote_copy(
            src_ref=src, dst_ref=dst, send_sem=s, recv_sem=r, device_id=device, device_id_type=MESH
        )

    def drain(ref, sem):
        pltpu.make_async_copy(ref, ref, sem).wait()

    barrier = pltpu.get_barrier_semaphore()
    others = 0
    for xx in (0, 1):
        ox = (x + xx) % NX
        for d in range(n):
            if xx == 0 and d == 0:
                continue
            pl.semaphore_signal(
                barrier, inc=1, device_id=dev(role, z, ox, (y + d) % n, tp), device_id_type=MESH
            )
            others += 1
            if d:
                pl.semaphore_signal(
                    barrier, inc=1, device_id=dev(role, (z + d) % n, ox, y, tp), device_id_type=MESH
                )
                others += 1
    peers = [((role + (k >> 1)) % 2, (tp + (k & 1)) % 2) for k in range(4)]
    for k in (1, 2, 3):
        pl.semaphore_signal(
            barrier, inc=1, device_id=dev(peers[k][0], z, x, y, peers[k][1]), device_id_type=MESH
        )
        others += 1
    pl.semaphore_signal(
        barrier, inc=1, device_id=dev(1 - role, z, 1 - x, y, tp), device_id_type=MESH
    )
    others += 1
    pl.semaphore_wait(barrier, others)

    @pl.when(role == 1)
    def _():
        xf = tok[...].astype(F32)
        inv = lax.rsqrt(jnp.mean(xf * xf, axis=1, keepdims=True) + EPSILON)
        lanes = lax.broadcasted_iota(jnp.int32, (8, 128), 1)
        comb = jnp.zeros((8, 128), F32)
        for k in range(ids.shape[1]):
            comb = comb + jnp.where(lanes == ids[:, k : k + 1], wts[:, k : k + 1], 0.0)
        for r in (0, 1):
            cols = pl.ds(pl.multiple_of((2 * r + tp) * ds, 128), ds)
            part = (tok[:, cols].astype(F32) * inv * gain[:, cols]).astype(BF)
            if r == 0:
                xsend[:, :ds] = part
                xsend[:, ds:] = comb.astype(BF)
            else:
                xpair[x, :, :ds] = part
                xpair[x, :, ds:] = comb.astype(BF)
        rcopy(xsend, xpair.at[x], snd.at[0], a0r.at[0], dev(0, z, x, y, tp)).start()
        rcopy(xsend, xpair.at[x], snd.at[1], a0r.at[1], dev(0, z, 1 - x, y, tp)).start()
        rcopy(xpair.at[x], xpair.at[x], snd.at[2], a0r.at[1], dev(1, z, 1 - x, y, tp)).start()

    def latent_send():
        for a in range(na):
            ts[a] = tok[:, a * fa : (a + 1) * fa]
        for d in range(1, na):
            ap = (a_me + d) % na
            rcopy(ts.at[ap], tr.at[a_me], snd.at[3], one.at[0], dev(role, ap // NX, ap % NX, y, tp)).start()
        for d in range(1, n):
            rcopy(kvw, wb.at[role, y], snd.at[4], one.at[1], dev(role, z, x, (y + d) % n, tp)).start()
        tr[a_me] = ts[a_me]
        wb[role, y] = kvw[...]

    def latent_swap():
        drain(wb.at[role, 0 : n - 1], one.at[1])
        rcopy(wb.at[role], wb.at[role], snd.at[5], one.at[2], dev(1 - role, z, x, y, tp)).start()

    def latent_project():
        drain(tr.at[0 : na - 1], one.at[0])
        drain(wb.at[0], one.at[2])
        rows = lax.broadcasted_iota(jnp.int32, (kc, 2 * kc), 0)
        cols = lax.broadcasted_iota(jnp.int32, (kc, 2 * kc), 1)
        weight = jnp.zeros((fa, 2 * kc), F32)
        for r in (0, 1):
            place = jnp.where(cols == rows + r * kc, 1.0, 0.0).astype(BF)
            block = wb[r].astype(F32).reshape(fa, kc).astype(BF)
            weight = weight + jnp.dot(block, place, preferred_element_type=F32)
        tokens = tr[...].astype(F32).reshape(na * 8, fa).astype(BF)
        share = jnp.dot(tokens, weight.astype(BF), preferred_element_type=F32)
        pk[...] = share.reshape(na, 8, 2 * kc)
        for d in range(1, na):
            ap = (a_me + d) % na
            rcopy(pk.at[ap], pkr.at[a_me], snd.at[6], one.at[3], dev(role, ap // NX, ap % NX, y, tp)).start()
        pkr[a_me] = pk[a_me]

    def latent_sum():
        drain(pkr.at[0 : na - 1], one.at[3])
        raw = jnp.sum(pkr[...], axis=0).astype(BF)

        @pl.when(role == 1)
        def _():
            rn[tp] = raw
            for k in (1, 2, 3):
                rcopy(
                    rn.at[tp], rn.at[tp], snd.at[7], k5n.at[tp], dev(peers[k][0], z, x, y, peers[k][1])
                ).start()

        @pl.when(role == 0)
        def _():
            ry[y] = raw
            for d in range(1, n):
                rcopy(ry.at[y], ry.at[y], snd.at[8], one.at[4], dev(role, z, x, (y + d) % n, tp)).start()

    def handoff_send():
        @pl.when(role == 0)
        def _():
            drain(ry.at[0 : n - 1], one.at[4])
            for a in range(na):
                rzs[a] = ry[sel[0, a]]
            for d in range(1, na):
                ap = (a_me + d) % na
                rcopy(rzs.at[ap], rz.at[a_me], snd.at[9], one.at[5], dev(role, ap // NX, ap % NX, y, tp)).start()
            rz[a_me] = rzs[a_me]

    def handoff_share():
        @pl.when(role == 0)
        def _():
            drain(rz.at[0 : na - 1], one.at[5])
            rp[tp] = rz[asrc[0, 0]]
            for k in (1, 2, 3):
                rcopy(
                    rp.at[tp], rp.at[tp], snd.at[10], k7r.at[tp], dev(peers[k][0], z, x, y, peers[k][1])
                ).start()

    def raw_rows():
        for t in (0, 1):
            @pl.when(jnp.logical_not(jnp.logical_and(role == 1, tp == t)))
            def _():
                drain(rn.at[t], k5n.at[t])

            @pl.when(jnp.logical_not(jnp.logical_and(role == 0, tp == t)))
            def _():
                drain(rp.at[t], k7r.at[t])

        rows = lax.broadcasted_iota(jnp.int32, (2 * kc, 4 * kc), 0)
        cols = lax.broadcasted_iota(jnp.int32, (2 * kc, 4 * kc), 1)
        new = jnp.zeros((8, 4 * kc), F32)
        prompt = jnp.zeros((8, 4 * kc), F32)
        for t in (0, 1):
            target = rows + t * kc + jnp.where(rows >= kc, kc, 0)
            place = jnp.where(cols == target, 1.0, 0.0).astype(BF)
            new = new + jnp.dot(rn[t], place, preferred_element_type=F32)
            prompt = prompt + jnp.dot(rp[t], place, preferred_element_type=F32)
        new_out[...] = new
        prompt_out[...] = prompt

    h_me = (y + z) % 2
    j_me = jnp.where(h_me == 0, y // 2, z // 2)

    def neighbour(h, step):
        if h == 0:
            return dev(role, (z + step) % n, x, y, tp)
        return dev(role, z, x, (y + step) % n, tp)

    def gather_start():
        @pl.when(role == 0)
        def _():
            drain(xpair.at[0], a0r.at[0])

        drain(xpair.at[0], a0r.at[1])
        pair = jnp.concatenate([xpair[0].astype(F32), xpair[1].astype(F32)], axis=0)
        xg[h_me, j_me] = pair.astype(BF)
        for d in range(1, n):
            where = dev(role, (z + d * h_me) % n, x, (y + d * (1 - h_me)) % n, tp)
            rcopy(xg.at[h_me, j_me], xg.at[h_me, j_me], snd.at[11], a1r.at[h_me, j_me], where).start()

    def own_or(h, j, yes, no):
        mine = jnp.logical_and(h_me == h, j_me == j)
        pl.when(jnp.logical_not(mine))(no)
        if yes is not None:
            pl.when(mine)(yes)

    def gather_step(s):
        for j in range(ch):
            for h in (0, 1):
                for d in (0, 1):
                    reach = half - d
                    if s == 0:
                        if d == 0:
                            own_or(h, j, None, lambda: drain(xg.at[h, j], a1r.at[h, j]))
                        here = xg.at[h, j]
                    else:
                        if s > reach:
                            continue
                        here = xg.at[slot(s, h, d), j]
                        drain(here, a2r.at[slot(s, h, d), j])
                    if s + 1 <= reach:
                        nxt = slot(s + 1, h, d)
                        rcopy(
                            here, xg.at[nxt, j], snd.at[12], a2r.at[nxt, j], neighbour(h, 1 - 2 * d)
                        ).start()

    def span(s):
        lo = slot(s, 0, 0)
        hi = slot(s + 1, 0, 0) if s < half else n_sets
        return lo, hi

    def project_step(s):
        lo, hi = span(s)
        m = (hi - lo) * ch * 16
        r0 = lo * ch * 16
        q = m // 4
        rows = xg[lo:hi].reshape(m, ds + 128)
        share = jnp.dot(rows[:, :ds], gu[...], preferred_element_type=F32)
        pf[r0 : r0 + m] = share
        ps[r0 : r0 + m] = share.astype(BF)
        for k in (1, 2, 3):
            there = pl.ds(pl.multiple_of(r0 + (peers[k][0] * 2 + peers[k][1]) * q, q), q)
            rcopy(
                ps.at[there], pr.at[k - 1, r0 // 4 : r0 // 4 + q], snd.at[13], b1r.at[s, k - 1],
                dev(peers[k][0], z, x, y, peers[k][1]),
            ).start()

    def hidden_step(s):
        lo, hi = span(s)
        m = (hi - lo) * ch * 16
        r0 = lo * ch * 16
        q = m // 4
        mine = pl.ds(pl.multiple_of(r0 + group * q, q), q)
        total = pf[mine]
        for k in (1, 2, 3):
            part = pr.at[k - 1, r0 // 4 : r0 // 4 + q]
            drain(part, b1r.at[s, k - 1])
            total = total + part[...].astype(F32)
        width = total.shape[1] // 2
        gate = total[:, :width]
        hb[mine] = (gate / (1.0 + jnp.exp(-gate)) * total[:, width:]).astype(BF)
        for k in (1, 2, 3):
            rcopy(
                hb.at[mine], hb.at[mine], snd.at[14], b2r.at[s, k - 1],
                dev(peers[k][0], z, x, y, peers[k][1]),
            ).start()

    def down_step(s):
        lo, hi = span(s)
        m = (hi - lo) * ch * 16
        r0 = lo * ch * 16
        q = m // 4
        for k in (1, 2, 3):
            drain(hb.at[0:q], b2r.at[s, k - 1])
        part = jnp.dot(hb[r0 : r0 + m], dn[...], preferred_element_type=F32)
        lanes = lax.broadcasted_iota(jnp.int32, (m, 128), 1)
        table = xg[lo:hi].reshape(m, ds + 128)[:, ds:].astype(F32)
        weight = jnp.sum(jnp.where(lanes == a_me, table, 0.0), axis=1, keepdims=True)
        out[lo:hi] = (part * weight).astype(BF).reshape(hi - lo, ch, 16, ds)

    def cslot(s, h, d):
        if s == 0:
            return h if d == 0 else n_sets + h
        return slot(s, h, d)

    def sum_step(s):
        for j in range(ch):
            for h in (0, 1):
                for d in (0, 1):
                    reach = half - d
                    if s > reach:
                        continue
                    if s == reach:
                        here = out.at[slot(s, h, d), j]
                    else:
                        here = cr.at[cslot(s, h, d), j]
                        drain(here, c2r.at[cslot(s, h, d), j])
                        here[...] = (
                            here[...].astype(F32) + out[slot(s, h, d), j].astype(F32)
                        ).astype(BF)
                    to = cslot(s - 1, h, d)
                    rcopy(
                        here, cr.at[to, j], snd.at[15], c2r.at[to, j], neighbour(h, 2 * d - 1)
                    ).start()

    def deliver():
        for j in range(ch):
            for h in (0, 1):
                total = out[h, j].astype(F32)
                for d in (0, 1):
                    if half - d < 1:
                        continue
                    here = cr.at[cslot(0, h, d), j]
                    drain(here, c2r.at[cslot(0, h, d), j])
                    total = total + here[...].astype(F32)
                if h == 0:
                    zz, yy, at = z, 2 * j + z % 2, y * NX + x
                else:
                    zz, yy, at = 2 * j + (1 - y % 2), y, z * NX + x
                for xd in (0, 1):
                    piece = fs.at[h, j, xd]
                    piece[...] = total[8 * xd : 8 * xd + 8].astype(BF)
                    itself = jnp.logical_and(jnp.logical_and(h_me == h, j_me == j), x == xd)

                    @pl.when(itself)
                    def _():
                        cf[at] = piece[...]

                    @pl.when(jnp.logical_not(itself))
                    def _():
                        rcopy(
                            piece, cf.at[at], snd.at[16], one.at[6], dev(role, zz, xd, yy, tp)
                        ).start()

    latent_send()
    gather_start()
    latent_swap()
    gather_step(0)
    latent_project()
    project_step(0)
    for s in range(1, half + 1):
        gather_step(s)
        if s == 1:
            latent_sum()
        if s == 2:
            handoff_send()
        if s == 3:
            handoff_share()
        project_step(s)
        hidden_step(s - 1)
        if s >= 2:
            down_step(s - 2)
    hidden_step(half)
    down_step(half - 1)
    down_step(half)
    for s in range(half, 0, -1):
        sum_step(s)
    deliver()
    raw_rows()
    drain(cf.at[0 : 2 * n - 1], one.at[6])
    moe_out[...] = jnp.sum(cf[...].astype(F32), axis=0).astype(BF)

    @pl.when(role == 1)
    def _():
        for i in (0, 1, 2):
            drain(xsend, snd.at[i])
        drain(rz.at[0:3], snd.at[7])

    @pl.when(role == 0)
    def _():
        drain(ry.at[0 : n - 1], snd.at[8])
        drain(rz.at[0 : na - 1], snd.at[9])
        drain(rz.at[0:3], snd.at[10])

    drain(tr.at[0 : na - 1], snd.at[3])
    drain(wb.at[0, 0 : n - 1], snd.at[4])
    drain(wb.at[0], snd.at[5])
    drain(pkr.at[0 : na - 1], snd.at[6])
    drain(xg.at[0 : n - 1, 0], snd.at[11])
    drain(xg.at[0 : 2 * (n - 1)], snd.at[12])
    rows = ps.shape[0] // 4 * 3
    drain(ps.at[0:rows], snd.at[13])
    drain(hb.at[0:rows], snd.at[14])
    drain(cr.at[0 : 2 * (n - 1)], snd.at[15])
    drain(cf.at[0 : 2 * n - 1], snd.at[16])


def fused(n, tok, gain, ids, wts, gu, dn, kvw, sel, asrc):
    half = n // 2
    ch = n // 2
    n_sets = 2 + (half - 1) * 4 + 2
    total_rows = n_sets * ch * 16
    ds, f2 = gu.shape
    dsx = ds + 128
    fe, kc = kvw.shape
    na = NX * n
    vm = pl.BlockSpec(memory_space=pltpu.VMEM)
    sm = pl.BlockSpec(memory_space=pltpu.SMEM)
    dma = pltpu.SemaphoreType.DMA
    scratch = [
        pltpu.VMEM((8, dsx), BF),
        pltpu.VMEM((2, 8, dsx), BF),
        pltpu.VMEM((n_sets, ch, 16, dsx), BF),
        pltpu.VMEM((total_rows, f2), F32),
        pltpu.VMEM((total_rows, f2), BF),
        pltpu.VMEM((3, total_rows // 4, f2), BF),
        pltpu.VMEM((total_rows, f2 // 2), BF),
        pltpu.VMEM((n_sets, ch, 16, ds), BF),
        pltpu.VMEM((n_sets + 2, ch, 16, ds), BF),
        pltpu.VMEM((2, ch, 2, 8, ds), BF),
        pltpu.VMEM((2 * n, 8, ds), BF),
        pltpu.VMEM((na, 8, n * fe), BF),
        pltpu.VMEM((na, 8, n * fe), BF),
        pltpu.VMEM((2, n, fe, kc), BF),
        pltpu.VMEM((na, 8, 2 * kc), F32),
        pltpu.VMEM((na, 8, 2 * kc), F32),
        pltpu.VMEM((2, 8, 2 * kc), BF),
        pltpu.VMEM((n, 8, 2 * kc), BF),
        pltpu.VMEM((na, 8, 2 * kc), BF),
        pltpu.VMEM((na, 8, 2 * kc), BF),
        pltpu.VMEM((2, 8, 2 * kc), BF),
        dma((2,)),
        dma((2, ch)),
        dma((n_sets, ch)),
        dma((half + 1, 3)),
        dma((half + 1, 3)),
        dma((n_sets + 2, ch)),
        dma((2,)),
        dma((2,)),
        dma((7,)),
        dma((17,)),
    ]
    return pl.pallas_call(
        functools.partial(fused_kernel, n),
        out_shape=(
            jax.ShapeDtypeStruct((8, ds), BF),
            jax.ShapeDtypeStruct((8, 4 * kc), F32),
            jax.ShapeDtypeStruct((8, 4 * kc), F32),
        ),
        in_specs=[vm] * 7 + [sm] * 2,
        out_specs=(vm, vm, vm),
        scratch_shapes=scratch,
        compiler_params=pltpu.CompilerParams(
            collective_id=0, has_side_effects=True, vmem_limit_bytes=56 * 1024 * 1024
        ),
    )(tok, gain, ids, wts, gu, dn, kvw, sel, asrc)


def per_device(
    n,
    pool_rows,
    kv_weight,
    kv_gain,
    latent_cache,
    queries,
    cache_lengths,
    partner,
    expert_ids,
    expert_weights,
    moe_gain,
    gate_up,
    down_proj,
):
    row_count = latent_cache.shape[0]
    ep = lax.axis_index("ep")
    names = jnp.arange(partner.shape[0], dtype=jnp.int32)
    wanted = jnp.arange(NX * n, dtype=jnp.int32) * n + ep % n
    source = jnp.sum(jnp.where(partner[None, :] == wanted[:, None], names[None, :], 0), axis=1)
    here = jnp.sum(jnp.where(partner == ep, names, 0))
    moe_out, new_raw, prompt_raw = fused(
        n,
        pool_rows[0],
        moe_gain[None, :],
        expert_ids,
        expert_weights,
        gate_up[0],
        down_proj[0],
        kv_weight,
        (source % n)[None, :],
        (here // n)[None, None],
    )
    leading = (jnp.arange(row_count, dtype=jnp.int32) == 0).astype(jnp.int32)
    new_keys = make_keys(new_raw, cache_lengths + row_count * leading, kv_gain)
    prompt_keys = make_keys(
        prompt_raw, cache_lengths[0] + jnp.arange(row_count, dtype=jnp.int32), kv_gain
    )
    attention_out = attend(queries, latent_cache, cache_lengths, prompt_keys, new_keys)
    return (attention_out, moe_out)


def solution(mesh):
    n = round((mesh.shape["ep"] // NX) ** 0.5)
    in_specs = (
        P("role", "ep", None),
        P("ep", ("role", "tp")),
        P(),
        P("ep", None, None),
        P("ep", ("role", "tp"), None),
        P("ep"),
        P(),
        P("ep", None),
        P("ep", None),
        P(),
        P("ep", ("role", "tp"), None),
        P("ep", None, ("role", "tp")),
    )
    out_specs = (P("ep", ("role", "tp"), None), P("ep", ("role", "tp")))
    return jax.shard_map(
        functools.partial(per_device, n),
        mesh=mesh, in_specs=in_specs, out_specs=out_specs, check_vma=False,
    )
```

time: 1340 us -> 117 us (0.09)
  the two profiles are of different devices: /device:TPU:4 before, /device:TPU:66 now
where the time goes in v1:
time: 117 us; the launch traced here: 116 us
  Pallas kernels  101 us (86%)
  other arithmetic  6.85 us (6%)
  between operations  3.39 us (3%)
  local copies, waits for them, and re-layouts  2.82 us (2%)
  matrix products  2.23 us (2%)
    pallas_call x1, Pallas kernels, fused(): pl.pallas_call(functools.partial(fused_kernel, n), out_shape=(jax.ShapeDt...  101 us

profile of v1, /device:TPU:66, one launch (start us, length us, event | category | flops | bytes accessed | tf_op | source)
XLA Modules:
  0.0 116.0 jit_solution(9264343851977361243)
XLA Ops:
  0.6 0.0 copy-start
  0.6 0.0 copy-start.3
  0.7 1.3 %fusion.35 = s32[]{:T(128)} fusion(s32[128]{0:T(128)} %param.18, s32[]{:T(128)S(6)} %axis_index.15), kind=kLoop, calls=%fused_computation.64 | loop fusion | flops 383 | bytes 520 | tf_op jit(solution)/shard_map/reduce_sum | solution.py:549
  4.6 0.8 select_reduce_fusion
  5.5 0.5 and_select_fusion.sel
  6.0 0.6 add_convert_fusion.1
  6.6 0.7 add_convert_fusion
  7.3 0.7 iota_compare_fusion
  8.1 0.0 copy-start.1
  8.1 100.7 %shard_map.131 = (bf16[8,1792]{1,0:T(8,128)(2,1)}, f32[8,576]{1,0:T(8,128)}, f32[8,576]{1,0:T(8,128)}) custom-call(bf16[8,7168]{1,0:T(8,128)(2,1)} %bitcast.35, f32[1,7168]{1,0:T(1,128)} %bitcast.38, s32[8,8]{1,0:T(8,128)} %ids.1, f32[8,8]{1,0:T(8,128)} %wts.1, bf16[1792,512]{1,0:T(8,128)(2,1)} %bitcast.31, bf16[256,1792]{1,0:T(8,128)(2,1)} %bitcast.32, ...), custom_call_target="tpu_custom_call" | custom-call | tf_op jit(solution)/shard_map/pallas_call | solution.py:513
  108.8 0.9 multiply_reduce_fusion
  109.7 0.7 slice.38
  110.4 0.7 slice.44
  111.1 0.0 copy-done.3
  111.1 0.8 fusion.38
  111.9 0.1 copy.37
  112.0 0.1 copy.47
  112.1 0.1 copy.46
  112.1 0.1 copy.32
  112.2 0.1 copy.45
  112.3 0.1 copy.44
  112.4 0.1 fusion.27
  112.5 0.1 copy.35
  112.6 0.1 copy.36
  112.7 0.1 copy.40
  112.8 0.1 copy.41
  112.9 0.0 copy-done
  112.9 0.2 fusion.11
  113.1 0.0 copy-start.2
  113.1 0.4 fusion.42
  113.5 0.0 copy-done.1
  113.5 0.3 fusion.41
  113.9 0.2 fusion.7
  114.1 0.3 fusion.5
  114.4 1.0 fusion.1
  115.4 0.0 copy-done.2
  115.4 0.6 copy.51
  (12 shorter events, 0.2 us)
Async XLA Ops:
  0.6 112.3 %copy-start = (bf16[8,32,576]{2,1,0:T(8,128)(2,1)S(1)}, bf16[8,32,576]{2,1,0:T(8,128)(2,1)}, u32[]{:S(2)}) copy-start(bf16[8,32,576]{2,1,0:T(8,128)(2,1)} %param.16) | copy-start | bytes 884740
  0.6 110.4 %copy-start.3 = (f32[512]{0:T(512)S(1)}, f32[512]{0:T(512)}, u32[]{:S(2)}) copy-start(f32[512]{0:T(512)} %param.14) | copy-start | bytes 6148
  8.1 105.5 %copy-start.1 = (bf16[8,48,576]{2,1,0:T(8,128)(2,1)S(1)}, bf16[8,48,576]{2,1,0:T(8,128)(2,1)}, u32[]{:S(2)}) copy-start(bf16[8,48,576]{2,1,0:T(8,128)(2,1)} %param.15) | copy-start | bytes 1327108
  113.1 2.3 %copy-start.2 = (bf16[8,1792]{1,0:T(8,128)(2,1)S(1)}, bf16[8,1792]{1,0:T(8,128)(2,1)}, u32[]{:S(2)}) copy-start(bf16[8,1792]{1,0:T(8,128)(2,1)} %get-tuple-element.34) | copy-start | bytes 86020

commit v2 on v1

v2 whole, which is shorter than its diff:
```python
import functools
import math

import jax
import jax.numpy as jnp
from jax import lax
from jax.experimental import pallas as pl
from jax.experimental.pallas import tpu as pltpu
from jax.sharding import PartitionSpec as P

MESH = pl.DeviceIdType.MESH
BF = jnp.bfloat16
F32 = jnp.float32
LATENT = 512
ROPE = 64
NOPE = 128
NX = 2
EPSILON = 1e-06


def fused_kernel(
    n, tok, gain, ids, wts, part, kvg, lens, kvw, gu_hbm, dn_hbm, q_hbm, cache_hbm,
    att, moe_out,
    gu, dn, qv, kb,
    xsend, xpair, xg, pf, ps, pr, hb, out, cr, fs, cf,
    ts, tr, wb, pk, pkr, rn, ry, rzs, rz, rp, kx,
    a0r, a1r, a2r, b1r, b2r, c2r, k5n, k7r, one, snd, loc,
):
    role, ep, tp = lax.axis_index("role"), lax.axis_index("ep"), lax.axis_index("tp")
    z, x, y = ep // (NX * n), (ep // n) % NX, ep % n
    a_me = ep // n
    na = NX * n
    ch = n // 2
    cd = ch // 2
    ds = gu.shape[0]
    fe, kc = kvw.shape
    fa = n * fe
    group = role * 2 + tp

    def dev(r, zz, xx, yy, t):
        return (r, (zz * NX + xx) * n + yy, t)

    def rcopy(src, dst, s, r, device):
        return pltpu.make_async_remote_copy(
            src_ref=src, dst_ref=dst, send_sem=s, recv_sem=r, device_id=device, device_id_type=MESH
        )

    def drain(ref, sem):
        pltpu.make_async_copy(ref, ref, sem).wait()

    barrier = pltpu.get_barrier_semaphore()
    others = 0
    for xx in (0, 1):
        ox = (x + xx) % NX
        for d in range(n):
            if xx == 0 and d == 0:
                continue
            pl.semaphore_signal(
                barrier, inc=1, device_id=dev(role, z, ox, (y + d) % n, tp), device_id_type=MESH
            )
            others += 1
            if d:
                pl.semaphore_signal(
                    barrier, inc=1, device_id=dev(role, (z + d) % n, ox, y, tp), device_id_type=MESH
                )
                others += 1
    peers = [((role + (k >> 1)) % 2, (tp + (k & 1)) % 2) for k in range(4)]
    for k in (1, 2, 3):
        pl.semaphore_signal(
            barrier, inc=1, device_id=dev(peers[k][0], z, x, y, peers[k][1]), device_id_type=MESH
        )
        others += 1
    pl.semaphore_signal(
        barrier, inc=1, device_id=dev(1 - role, z, 1 - x, y, tp), device_id_type=MESH
    )
    others += 1

    load_gu = pltpu.make_async_copy(gu_hbm.at[0], gu, loc.at[0])
    load_dn = pltpu.make_async_copy(dn_hbm.at[0], dn, loc.at[1])
    load_q = pltpu.make_async_copy(q_hbm, qv, loc.at[2])
    load_cache = pltpu.make_async_copy(cache_hbm, kb.at[:, 0 : cache_hbm.shape[1]], loc.at[3])
    load_gu.start()
    load_dn.start()
    load_q.start()
    load_cache.start()

    @pl.when(role == 1)
    def _():
        xf = tok[0].astype(F32)
        inv = lax.rsqrt(jnp.mean(xf * xf, axis=1, keepdims=True) + EPSILON)
        lanes = lax.broadcasted_iota(jnp.int32, (8, 128), 1)
        comb = jnp.zeros((8, 128), F32)
        for k in range(ids.shape[1]):
            comb = comb + jnp.where(lanes == ids[:, k : k + 1], wts[:, k : k + 1], 0.0)
        for r in (0, 1):
            cols = pl.ds(pl.multiple_of((2 * r + tp) * ds, 128), ds)
            scaled = (tok[0, :, cols].astype(F32) * inv * gain[:, cols]).astype(BF)
            if r == 0:
                xsend[:, :ds] = scaled
                xsend[:, ds:] = comb.astype(BF)
            else:
                xpair[x, :, :ds] = scaled
                xpair[x, :, ds:] = comb.astype(BF)

    pl.semaphore_wait(barrier, others)

    @pl.when(role == 1)
    def _():
        rcopy(xsend, xpair.at[x], snd.at[1], a0r.at[1], dev(0, z, 1 - x, y, tp)).start()
        rcopy(xpair.at[x], xpair.at[x], snd.at[2], a0r.at[1], dev(1, z, 1 - x, y, tp)).start()
        rcopy(xsend, xpair.at[x], snd.at[0], a0r.at[0], dev(0, z, x, y, tp)).start()

    def latent_send():
        for a in range(na):
            ts[a] = tok[0, :, a * fa : (a + 1) * fa]
        for d in range(1, na):
            ap = (a_me + d) % na
            rcopy(ts.at[ap], tr.at[a_me], snd.at[3], one.at[0], dev(role, ap // NX, ap % NX, y, tp)).start()
        for d in range(1, n):
            rcopy(kvw, wb.at[role, y], snd.at[4], one.at[1], dev(role, z, x, (y + d) % n, tp)).start()
        tr[a_me] = ts[a_me]
        wb[role, y] = kvw[...]

    def latent_swap():
        drain(wb.at[role, 0 : n - 1], one.at[1])
        rcopy(wb.at[role], wb.at[role], snd.at[5], one.at[2], dev(1 - role, z, x, y, tp)).start()

    def latent_project():
        drain(tr.at[0 : na - 1], one.at[0])
        drain(wb.at[0], one.at[2])
        rows = lax.broadcasted_iota(jnp.int32, (kc, 2 * kc), 0)
        cols = lax.broadcasted_iota(jnp.int32, (kc, 2 * kc), 1)
        weight = jnp.zeros((fa, 2 * kc), F32)
        for r in (0, 1):
            place = jnp.where(cols == rows + r * kc, 1.0, 0.0).astype(BF)
            block = wb[r].astype(F32).reshape(fa, kc).astype(BF)
            weight = weight + jnp.dot(block, place, preferred_element_type=F32)
        tokens = tr[...].astype(F32).reshape(na * 8, fa).astype(BF)
        share = jnp.dot(tokens, weight.astype(BF), preferred_element_type=F32)
        pk[...] = share.reshape(na, 8, 2 * kc)
        for d in range(1, na):
            ap = (a_me + d) % na
            rcopy(pk.at[ap], pkr.at[a_me], snd.at[6], one.at[3], dev(role, ap // NX, ap % NX, y, tp)).start()
        pkr[a_me] = pk[a_me]

    def latent_sum():
        drain(pkr.at[0 : na - 1], one.at[3])
        raw = jnp.sum(pkr[...], axis=0).astype(BF)

        @pl.when(role == 1)
        def _():
            rn[tp] = raw
            for k in (1, 2, 3):
                rcopy(
                    rn.at[tp], rn.at[tp], snd.at[7], k5n.at[tp], dev(peers[k][0], z, x, y, peers[k][1])
                ).start()

        @pl.when(role == 0)
        def _():
            ry[y] = raw
            for d in range(1, n):
                rcopy(ry.at[y], ry.at[y], snd.at[8], one.at[4], dev(role, z, x, (y + d) % n, tp)).start()

    def handoff_send():
        @pl.when(role == 0)
        def _():
            drain(ry.at[0 : n - 1], one.at[4])
            p_at = lax.broadcasted_iota(jnp.int32, (na * n, n * 8), 0)
            l_at = lax.broadcasted_iota(jnp.int32, (na * n, n * 8), 1)
            pick = jnp.where(p_at == a_me * n + l_at // 8, 1.0, 0.0).astype(BF)
            names = jnp.broadcast_to(part[...].astype(F32), (8, na * n)).astype(BF)
            dest = jnp.dot(names, pick, preferred_element_type=F32)[0:1]
            r_at = lax.broadcasted_iota(jnp.int32, (na * 8, n * 8), 0)
            c_at = lax.broadcasted_iota(jnp.int32, (na * 8, n * 8), 1)
            wanted = (r_at // 8 * n + y).astype(F32)
            move = jnp.where(
                jnp.logical_and(wanted == dest, r_at % 8 == c_at % 8), 1.0, 0.0
            ).astype(BF)
            held = ry[...].astype(F32).reshape(n * 8, 2 * kc).astype(BF)
            moved = jnp.dot(move, held, preferred_element_type=F32)
            rzs[...] = moved.reshape(na, 8, 2 * kc).astype(BF)
            for d in range(1, na):
                ap = (a_me + d) % na
                rcopy(rzs.at[ap], rz.at[a_me], snd.at[9], one.at[5], dev(role, ap // NX, ap % NX, y, tp)).start()
            rz[a_me] = rzs[a_me]

    def handoff_share():
        @pl.when(role == 0)
        def _():
            drain(rz.at[0 : na - 1], one.at[5])
            rp[tp] = jnp.sum(rz[...].astype(F32), axis=0).astype(BF)
            for k in (1, 2, 3):
                rcopy(
                    rp.at[tp], rp.at[tp], snd.at[10], k7r.at[tp], dev(peers[k][0], z, x, y, peers[k][1])
                ).start()

    def make_keys():
        for t in (0, 1):
            @pl.when(jnp.logical_not(jnp.logical_and(role == 1, tp == t)))
            def _():
                drain(rn.at[t], k5n.at[t])

            @pl.when(jnp.logical_not(jnp.logical_and(role == 0, tp == t)))
            def _():
                drain(rp.at[t], k7r.at[t])

        rows = lax.broadcasted_iota(jnp.int32, (2 * kc, 4 * kc), 0)
        cols = lax.broadcasted_iota(jnp.int32, (2 * kc, 4 * kc), 1)
        raw = jnp.zeros((16, 4 * kc), F32)
        for t in (0, 1):
            target = rows + t * kc + jnp.where(rows >= kc, kc, 0)
            place = jnp.where(cols == target, 1.0, 0.0).astype(BF)
            both = jnp.concatenate([rp[t].astype(F32), rn[t].astype(F32)], axis=0).astype(BF)
            raw = raw + jnp.dot(both, place, preferred_element_type=F32)
        latent = raw[:, :LATENT]
        inv = lax.rsqrt(jnp.mean(latent * latent, axis=1, keepdims=True) + EPSILON)
        rotary = raw[:, LATENT:]
        at0 = lax.broadcasted_iota(jnp.int32, (ROPE, ROPE), 0)
        at1 = lax.broadcasted_iota(jnp.int32, (ROPE, ROPE), 1)
        swap = jnp.where(at0 == at1 + 1 - 2 * (at1 % 2), 1.0, 0.0).astype(BF)
        swapped = jnp.dot(rotary.astype(BF), swap, preferred_element_type=F32)
        row = lax.broadcasted_iota(jnp.int32, (16, ROPE), 0)
        lane = lax.broadcasted_iota(jnp.int32, (16, ROPE), 1)
        position = jnp.where(row < 8, row + lens[0], 0)
        for b in range(8):
            position = position + jnp.where(row == 8 + b, lens[b] + (8 if b == 0 else 0), 0)
        frequency = jnp.exp((lane // 2).astype(F32) * (-2.0 / ROPE * math.log(10000.0)))
        angle = position.astype(F32) * frequency
        sign = jnp.where(lane % 2 == 0, -1.0, 1.0)
        turned = rotary * jnp.cos(angle) + swapped * sign * jnp.sin(angle)
        kx[:, :LATENT] = (latent * inv * kvg[...]).astype(BF)
        kx[:, LATENT:] = turned.astype(BF)

    def attend(b):
        count = cache_hbm.shape[1]
        kb[b, count : count + 16] = kx[...]
        score = lax.dot_general(
            qv[b], kb[b], (((1,), (1,)), ((), ())), preferred_element_type=F32
        ) * ((NOPE + ROPE) ** (-0.5))
        lane = lax.broadcasted_iota(jnp.int32, score.shape, 1)
        keep = jnp.logical_or(lane < lens[b], lane == count + 8 + b)
        if b == 0:
            keep = jnp.logical_or(keep, jnp.logical_and(lane >= count, lane < count + 8))
        score = jnp.where(keep, score, -jnp.inf)
        top = jnp.max(score, axis=1, keepdims=True)
        weight = jnp.exp(score - top)
        weight = (weight / jnp.sum(weight, axis=1, keepdims=True)).astype(BF)
        att[b] = jnp.dot(weight, kb[b, :, :LATENT], preferred_element_type=F32).astype(BF)

    h_me = (y + z) % 2
    j_me = jnp.where(h_me == 0, y // 2, z // 2)

    def neighbour(q):
        step = 1 - 2 * (q % 2)
        if q < 2:
            return dev(role, (z + step) % n, x, y, tp)
        return dev(role, z, x, (y + step) % n, tp)

    def gather_start():
        @pl.when(role == 0)
        def _():
            drain(xpair.at[0], a0r.at[0])

        drain(xpair.at[0], a0r.at[1])
        pair = jnp.concatenate([xpair[0].astype(F32), xpair[1].astype(F32)], axis=0)
        q_me, jj = 2 * h_me + j_me // cd, j_me % cd
        mine = xg.at[0, q_me, jj]
        mine[...] = pair.astype(BF)
        step = 1 - 2 * (j_me // cd)
        where = dev(role, (z + step * (1 - h_me)) % n, x, (y + step * h_me) % n, tp)
        rcopy(mine, xg.at[1, q_me, jj], snd.at[12], a2r.at[1, q_me, jj], where).start()
        for d in range(1, n):
            where = dev(role, (z + d * h_me) % n, x, (y + d * (1 - h_me)) % n, tp)
            rcopy(mine, mine, snd.at[11], a1r.at[q_me, jj], where).start()

    def gather_step(k):
        for jj in range(cd):
            for q in range(4):
                here = xg.at[k, q, jj]

                def forward():
                    drain(here, a2r.at[k, q, jj] if k else a1r.at[q, jj])
                    if k < n - 1:
                        rcopy(
                            here, xg.at[k + 1, q, jj], snd.at[12], a2r.at[k + 1, q, jj], neighbour(q)
                        ).start()

                if k:
                    forward()
                else:
                    j = (q % 2) * cd + jj
                    mine = jnp.logical_and(h_me == q // 2, j_me == j)
                    pl.when(jnp.logical_not(mine))(forward)

    step_rows = 4 * cd * 16
    quarter = cd * 16

    def project_step(k):
        if k == 0:
            load_gu.wait()
        rows = xg[k].reshape(step_rows, ds + 128)
        share = jnp.dot(rows[:, :ds], gu[...], preferred_element_type=F32)
        pf[k] = share
        ps[k] = share.astype(BF)
        for i in (1, 2, 3):
            there = pl.ds(pl.multiple_of((peers[i][0] * 2 + peers[i][1]) * quarter, quarter), quarter)
            rcopy(
                ps.at[k, there], pr.at[k, i - 1], snd.at[13], b1r.at[k, i - 1],
                dev(peers[i][0], z, x, y, peers[i][1]),
            ).start()

    def hidden_step(k):
        mine = pl.ds(pl.multiple_of(group * quarter, quarter), quarter)
        total = pf[k, mine]
        for i in (1, 2, 3):
            drain(pr.at[k, i - 1], b1r.at[k, i - 1])
            total = total + pr[k, i - 1].astype(F32)
        width = total.shape[1] // 2
        gate = total[:, :width]
        table = xg[k, group].reshape(quarter, ds + 128)[:, ds:].astype(F32)
        lanes = lax.broadcasted_iota(jnp.int32, (quarter, 128), 1)
        weight = jnp.sum(jnp.where(lanes == a_me, table, 0.0), axis=1, keepdims=True)
        hb[k, mine] = (gate / (1.0 + jnp.exp(-gate)) * total[:, width:] * weight).astype(BF)
        for i in (1, 2, 3):
            rcopy(
                hb.at[k, mine], hb.at[k, mine], snd.at[14], b2r.at[k, i - 1],
                dev(peers[i][0], z, x, y, peers[i][1]),
            ).start()

    def down_step(k):
        if k == 0:
            load_dn.wait()
        for i in (1, 2, 3):
            drain(hb.at[k, 0:quarter], b2r.at[k, i - 1])
        result = jnp.dot(hb[k], dn[...], preferred_element_type=F32)
        out[k] = result.astype(BF).reshape(4, cd, 16, ds)

    def sum_step(k):
        for jj in range(cd):
            for q in range(4):
                if k == 1:
                    here = out.at[k, q, jj]
                else:
                    here = cr.at[k - 2, q, jj]
                    drain(here, c2r.at[k - 2, q, jj])
                    here[...] = (here[...].astype(F32) + out[k, q, jj].astype(F32)).astype(BF)
                rcopy(
                    here, cr.at[k - 1, q, jj], snd.at[15], c2r.at[k - 1, q, jj], neighbour(q)
                ).start()

    def deliver():
        for jj in range(cd):
            for q in range(4):
                h, j = q // 2, (q % 2) * cd + jj
                here = cr.at[n - 2, q, jj]
                drain(here, c2r.at[n - 2, q, jj])
                total = out[0, q, jj].astype(F32) + here[...].astype(F32)
                if h == 0:
                    zz, yy, at = z, 2 * j + z % 2, y * NX + x
                else:
                    zz, yy, at = 2 * j + (1 - y % 2), y, z * NX + x
                for xd in (0, 1):
                    piece = fs.at[h, j, xd]
                    piece[...] = total[8 * xd : 8 * xd + 8].astype(BF)
                    itself = jnp.logical_and(jnp.logical_and(h_me == h, j_me == j), x == xd)

                    @pl.when(itself)
                    def _():
                        cf[at] = piece[...]

                    @pl.when(jnp.logical_not(itself))
                    def _():
                        rcopy(
                            piece, cf.at[at], snd.at[16], one.at[6], dev(role, zz, xd, yy, tp)
                        ).start()

    gather_start()
    latent_send()
    gather_step(0)
    project_step(0)
    latent_swap()
    for k in range(1, n):
        gather_step(k)
        project_step(k)
        hidden_step(k - 1)
        if k >= 2:
            down_step(k - 2)
        if k >= 3:
            sum_step(k - 2)
        if k == 1:
            latent_project()
        if k == 3:
            latent_sum()
        if k == 4:
            handoff_send()
        if k == 6:
            handoff_share()
    hidden_step(n - 1)
    down_step(n - 2)
    sum_step(n - 2)
    down_step(n - 1)
    sum_step(n - 1)
    load_q.wait()
    load_cache.wait()
    make_keys()
    for b in range(8):
        attend(b)
    deliver()
    drain(cf.at[0 : 2 * n - 1], one.at[6])
    moe_out[...] = jnp.sum(cf[...].astype(F32), axis=0).astype(BF)

    @pl.when(role == 1)
    def _():
        for i in (0, 1, 2):
            drain(xsend, snd.at[i])
        drain(rz.at[0:3], snd.at[7])

    @pl.when(role == 0)
    def _():
        drain(ry.at[0 : n - 1], snd.at[8])
        drain(rz.at[0 : na - 1], snd.at[9])
        drain(rz.at[0:3], snd.at[10])

    drain(tr.at[0 : na - 1], snd.at[3])
    drain(wb.at[0, 0 : n - 1], snd.at[4])
    drain(wb.at[0], snd.at[5])
    drain(pkr.at[0 : na - 1], snd.at[6])
    drain(xg.at[0 : n - 1, 0, 0], snd.at[11])
    drain(xg.at[0 : n - 1], snd.at[12])
    drain(pr, snd.at[13])
    drain(hb.at[:, 0 : 3 * quarter], snd.at[14])
    drain(cr, snd.at[15])
    drain(cf.at[0 : 2 * n - 1], snd.at[16])


def fused(n, tok, gain, ids, wts, part, kvg, lens, kvw, gu, dn, queries, cache):
    ch = n // 2
    cd = ch // 2
    step_rows = 4 * cd * 16
    _, ds, f2 = gu.shape
    dsx = ds + 128
    fe, kc = kvw.shape
    na = NX * n
    heads, width = queries.shape[1:]
    vm = pl.BlockSpec(memory_space=pltpu.VMEM)
    sm = pl.BlockSpec(memory_space=pltpu.SMEM)
    hbm = pl.BlockSpec(memory_space=pl.ANY)
    dma = pltpu.SemaphoreType.DMA
    scratch = [
        pltpu.VMEM((ds, f2), BF),
        pltpu.VMEM((f2 // 2, ds), BF),
        pltpu.VMEM((8, heads, width), BF),
        pltpu.VMEM((8, cache.shape[1] + 16, width), BF),
        pltpu.VMEM((8, dsx), BF),
        pltpu.VMEM((2, 8, dsx), BF),
        pltpu.VMEM((n, 4, cd, 16, dsx), BF),
        pltpu.VMEM((n, step_rows, f2), F32),
        pltpu.VMEM((n, step_rows, f2), BF),
        pltpu.VMEM((n, 3, step_rows // 4, f2), BF),
        pltpu.VMEM((n, step_rows, f2 // 2), BF),
        pltpu.VMEM((n, 4, cd, 16, ds), BF),
        pltpu.VMEM((n - 1, 4, cd, 16, ds), BF),
        pltpu.VMEM((2, ch, 2, 8, ds), BF),
        pltpu.VMEM((2 * n, 8, ds), BF),
        pltpu.VMEM((na, 8, n * fe), BF),
        pltpu.VMEM((na, 8, n * fe), BF),
        pltpu.VMEM((2, n, fe, kc), BF),
        pltpu.VMEM((na, 8, 2 * kc), F32),
        pltpu.VMEM((na, 8, 2 * kc), F32),
        pltpu.VMEM((2, 8, 2 * kc), BF),
        pltpu.VMEM((n, 8, 2 * kc), BF),
        pltpu.VMEM((na, 8, 2 * kc), BF),
        pltpu.VMEM((na, 8, 2 * kc), BF),
        pltpu.VMEM((2, 8, 2 * kc), BF),
        pltpu.VMEM((16, width), BF),
        dma((2,)),
        dma((4, cd)),
        dma((n, 4, cd)),
        dma((n, 3)),
        dma((n, 3)),
        dma((n - 1, 4, cd)),
        dma((2,)),
        dma((2,)),
        dma((7,)),
        dma((17,)),
        dma((4,)),
    ]
    return pl.pallas_call(
        functools.partial(fused_kernel, n),
        out_shape=(
            jax.ShapeDtypeStruct((8, heads, LATENT), BF),
            jax.ShapeDtypeStruct((8, ds), BF),
        ),
        in_specs=[vm] * 6 + [sm] + [vm] + [hbm] * 4,
        out_specs=(vm, vm),
        scratch_shapes=scratch,
        compiler_params=pltpu.CompilerParams(
            collective_id=0, has_side_effects=True, vmem_limit_bytes=56 * 1024 * 1024
        ),
    )(tok, gain, ids, wts, part, kvg, lens, kvw, gu, dn, queries, cache)


def per_device(
    n,
    pool_rows,
    kv_weight,
    kv_gain,
    latent_cache,
    queries,
    cache_lengths,
    partner,
    expert_ids,
    expert_weights,
    moe_gain,
    gate_up,
    down_proj,
):
    return fused(
        n,
        pool_rows,
        moe_gain[None, :],
        expert_ids,
        expert_weights,
        partner[None, :],
        kv_gain[None, :],
        cache_lengths,
        kv_weight,
        gate_up,
        down_proj,
        queries,
        latent_cache,
    )


def solution(mesh):
    n = round((mesh.shape["ep"] // NX) ** 0.5)
    in_specs = (
        P("role", "ep", None),
        P("ep", ("role", "tp")),
        P(),
        P("ep", None, None),
        P("ep", ("role", "tp"), None),
        P("ep"),
        P(),
        P("ep", None),
        P("ep", None),
        P(),
        P("ep", ("role", "tp"), None),
        P("ep", None, ("role", "tp")),
    )
    out_specs = (P("ep", ("role", "tp"), None), P("ep", ("role", "tp")))
    return jax.shard_map(
        functools.partial(per_device, n),
        mesh=mesh, in_specs=in_specs, out_specs=out_specs, check_vma=False,
    )
```

time: 117 us -> 96.3 us (0.82)
  the two profiles are of different devices: /device:TPU:66 before, /device:TPU:17 now
where the time goes in v2:
time: 96.3 us; the launch traced here: 96 us
  Pallas kernels  92.3 us (96%)
  local copies, waits for them, and re-layouts  3.03 us (3%)
    pallas_call x1, Pallas kernels, fused(): pl.pallas_call(functools.partial(fused_kernel, n), out_shape=(jax.ShapeDt...  92.3 us
    unnamed x2, local copies, waits for them, and re-layouts  3.03 us

profile of v2, /device:TPU:17, one launch (start us, length us, event | category | flops | bytes accessed | tf_op | source)
XLA Modules:
  0.0 96.0 jit_solution(17406256093242408732)
XLA Ops:
  0.6 92.3 %shard_map.131 = (bf16[8,32,512]{2,1,0:T(8,128)(2,1)}, bf16[8,1792]{1,0:T(8,128)(2,1)}) custom-call(bf16[1,8,7168]{2,1,0:T(8,128)(2,1)} %tok.1, f32[1,7168]{1,0:T(1,128)} %bitcast.3, s32[8,8]{1,0:T(8,128)} %ids.1, f32[8,8]{1,0:T(8,128)} %wts.1, s32[1,128]{1,0:T(1,128)} %bitcast.5, f32[1,512]{1,0:T(1,128)} %bitcast.4, s32[8]{0:T(128)} %lens.1, ...), custom_call_target="tpu_custom_call" | custom-call | tf_op jit(solution)/shard_map/pallas_call | solution.py:488
  93.0 1.7 %copy.16 = bf16[8,32,512]{2,1,0:T(8,128)(2,1)} copy(bf16[8,32,512]{2,1,0:T(8,128)(2,1)} %get-tuple-element.4) | data formatting | bytes 524288
  94.7 1.4 %copy.17 = bf16[8,1792]{1,0:T(8,128)(2,1)} copy(bf16[8,1792]{1,0:T(8,128)(2,1)} %get-tuple-element.5) | data formatting | bytes 57344

commit v3 on v2

--- a/solution.py
+++ b/solution.py
@@ -24,14 +24,13 @@
     gu, dn, qv, kb,
     xsend, xpair, xg, pf, ps, pr, hb, out, cr, fs, cf,
     ts, tr, wb, pk, pkr, rn, ry, rzs, rz, rp, kx,
-    a0r, a1r, a2r, b1r, b2r, c2r, k5n, k7r, one, snd, loc,
+    a0r, a1r, a2r, b1r, b2r, c2r, k5n, k7r, one, snd, loc, wr,
 ):
     role, ep, tp = lax.axis_index("role"), lax.axis_index("ep"), lax.axis_index("tp")
     z, x, y = ep // (NX * n), (ep // n) % NX, ep % n
     a_me = ep // n
     na = NX * n
     ch = n // 2
-    cd = ch // 2
     ds = gu.shape[0]
     fe, kc = kvw.shape
     fa = n * fe
@@ -102,6 +101,9 @@
                 xpair[x, :, :ds] = scaled
                 xpair[x, :, ds:] = comb.astype(BF)
 
+    for a in range(na):
+        ts[a] = tok[0, :, a * fa : (a + 1) * fa]
+
     pl.semaphore_wait(barrier, others)
 
     @pl.when(role == 1)
@@ -111,8 +113,6 @@
         rcopy(xsend, xpair.at[x], snd.at[0], a0r.at[0], dev(0, z, x, y, tp)).start()
 
     def latent_send():
-        for a in range(na):
-            ts[a] = tok[0, :, a * fa : (a + 1) * fa]
         for d in range(1, na):
             ap = (a_me + d) % na
             rcopy(ts.at[ap], tr.at[a_me], snd.at[3], one.at[0], dev(role, ap // NX, ap % NX, y, tp)).start()
@@ -137,7 +137,7 @@
             weight = weight + jnp.dot(block, place, preferred_element_type=F32)
         tokens = tr[...].astype(F32).reshape(na * 8, fa).astype(BF)
         share = jnp.dot(tokens, weight.astype(BF), preferred_element_type=F32)
-        pk[...] = share.reshape(na, 8, 2 * kc)
+        pk[...] = share.reshape(na, 8, 2 * kc).astype(BF)
         for d in range(1, na):
             ap = (a_me + d) % na
             rcopy(pk.at[ap], pkr.at[a_me], snd.at[6], one.at[3], dev(role, ap // NX, ap % NX, y, tp)).start()
@@ -145,7 +145,7 @@
 
     def latent_sum():
         drain(pkr.at[0 : na - 1], one.at[3])
-        raw = jnp.sum(pkr[...], axis=0).astype(BF)
+        raw = jnp.sum(pkr[...].astype(F32), axis=0).astype(BF)
 
         @pl.when(role == 1)
         def _():
@@ -248,7 +248,7 @@
         att[b] = jnp.dot(weight, kb[b, :, :LATENT], preferred_element_type=F32).astype(BF)
 
     h_me = (y + z) % 2
-    j_me = jnp.where(h_me == 0, y // 2, z // 2)
+    line = jnp.where(h_me == 0, y, z)
 
     def neighbour(q):
         step = 1 - 2 * (q % 2)
@@ -263,149 +263,140 @@
 
         drain(xpair.at[0], a0r.at[1])
         pair = jnp.concatenate([xpair[0].astype(F32), xpair[1].astype(F32)], axis=0)
-        q_me, jj = 2 * h_me + j_me // cd, j_me % cd
-        mine = xg.at[0, q_me, jj]
+        mine = xg.at[0, 0, 2 * h_me]
         mine[...] = pair.astype(BF)
-        step = 1 - 2 * (j_me // cd)
-        where = dev(role, (z + step * (1 - h_me)) % n, x, (y + step * h_me) % n, tp)
-        rcopy(mine, xg.at[1, q_me, jj], snd.at[12], a2r.at[1, q_me, jj], where).start()
-        for d in range(1, n):
+        where = dev(role, (z + 1 - h_me) % n, x, (y + h_me) % n, tp)
+        rcopy(mine, xg.at[1, 0, 2 * h_me], snd.at[12], a2r.at[1, 0, 2 * h_me], where).start()
+        for d in (1, n - 1, 2, n - 2, 3, n - 3, 4):
             where = dev(role, (z + d * h_me) % n, x, (y + d * (1 - h_me)) % n, tp)
-            rcopy(mine, mine, snd.at[11], a1r.at[q_me, jj], where).start()
-
-    def gather_step(k):
-        for jj in range(cd):
-            for q in range(4):
-                here = xg.at[k, q, jj]
-
-                def forward():
-                    drain(here, a2r.at[k, q, jj] if k else a1r.at[q, jj])
-                    if k < n - 1:
-                        rcopy(
-                            here, xg.at[k + 1, q, jj], snd.at[12], a2r.at[k + 1, q, jj], neighbour(q)
-                        ).start()
-
-                if k:
-                    forward()
-                else:
-                    j = (q % 2) * cd + jj
-                    mine = jnp.logical_and(h_me == q // 2, j_me == j)
-                    pl.when(jnp.logical_not(mine))(forward)
-
-    step_rows = 4 * cd * 16
-    quarter = cd * 16
-
-    def project_step(k):
-        if k == 0:
+            e = ((line + d) % n // 2 - line // 2 + ch) % ch
+            w, q = e // 2, 2 * h_me + e % 2
+            rcopy(mine, xg.at[0, w, q], snd.at[11], a1r.at[w, q], where).start()
+
+    def gather_step(k, w):
+        for q in range(4):
+            here = xg.at[k, w, q]
+
+            def forward():
+                drain(here, a2r.at[k, w, q] if k else a1r.at[w, q])
+                if k < n - 1:
+                    rcopy(
+                        here, xg.at[k + 1, w, q], snd.at[12], a2r.at[k + 1, w, q], neighbour(q)
+                    ).start()
+
+            if k == 0 and w == 0 and q % 2 == 0:
+                pl.when(h_me != q // 2)(forward)
+            else:
+                forward()
+
+    def project_step(k, w):
+        if k == 0 and w == 0:
             load_gu.wait()
-        rows = xg[k].reshape(step_rows, ds + 128)
+        rows = xg[k, w].reshape(64, ds + 128)
         share = jnp.dot(rows[:, :ds], gu[...], preferred_element_type=F32)
-        pf[k] = share
-        ps[k] = share.astype(BF)
+        pf[k, w] = share
+        ps[k, w] = share.astype(BF)
         for i in (1, 2, 3):
-            there = pl.ds(pl.multiple_of((peers[i][0] * 2 + peers[i][1]) * quarter, quarter), quarter)
+            there = pl.ds(pl.multiple_of((peers[i][0] * 2 + peers[i][1]) * 16, 16), 16)
             rcopy(
-                ps.at[k, there], pr.at[k, i - 1], snd.at[13], b1r.at[k, i - 1],
+                ps.at[k, w, there], pr.at[k, w, i - 1], snd.at[13], b1r.at[k, w, i - 1],
                 dev(peers[i][0], z, x, y, peers[i][1]),
             ).start()
 
-    def hidden_step(k):
-        mine = pl.ds(pl.multiple_of(group * quarter, quarter), quarter)
-        total = pf[k, mine]
+    def hidden_step(k, w):
+        mine = pl.ds(pl.multiple_of(group * 16, 16), 16)
+        total = pf[k, w, mine]
         for i in (1, 2, 3):
-            drain(pr.at[k, i - 1], b1r.at[k, i - 1])
-            total = total + pr[k, i - 1].astype(F32)
+            drain(pr.at[k, w, i - 1], b1r.at[k, w, i - 1])
+            total = total + pr[k, w, i - 1].astype(F32)
         width = total.shape[1] // 2
         gate = total[:, :width]
-        table = xg[k, group].reshape(quarter, ds + 128)[:, ds:].astype(F32)
-        lanes = lax.broadcasted_iota(jnp.int32, (quarter, 128), 1)
+        table = xg[k, w, group][:, ds:].astype(F32)
+        lanes = lax.broadcasted_iota(jnp.int32, (16, 128), 1)
         weight = jnp.sum(jnp.where(lanes == a_me, table, 0.0), axis=1, keepdims=True)
-        hb[k, mine] = (gate / (1.0 + jnp.exp(-gate)) * total[:, width:] * weight).astype(BF)
+        hb[k, w, mine] = (gate / (1.0 + jnp.exp(-gate)) * total[:, width:] * weight).astype(BF)
         for i in (1, 2, 3):
             rcopy(
-                hb.at[k, mine], hb.at[k, mine], snd.at[14], b2r.at[k, i - 1],
+                hb.at[k, w, mine], hb.at[k, w, mine], snd.at[14], b2r.at[k, w, i - 1],
                 dev(peers[i][0], z, x, y, peers[i][1]),
             ).start()
 
-    def down_step(k):
-        if k == 0:
+    def down_step(k, w):
+        if k == 0 and w == 0:
             load_dn.wait()
         for i in (1, 2, 3):
-            drain(hb.at[k, 0:quarter], b2r.at[k, i - 1])
-        result = jnp.dot(hb[k], dn[...], preferred_element_type=F32)
-        out[k] = result.astype(BF).reshape(4, cd, 16, ds)
-
-    def sum_step(k):
-        for jj in range(cd):
-            for q in range(4):
-                if k == 1:
-                    here = out.at[k, q, jj]
-                else:
-                    here = cr.at[k - 2, q, jj]
-                    drain(here, c2r.at[k - 2, q, jj])
-                    here[...] = (here[...].astype(F32) + out[k, q, jj].astype(F32)).astype(BF)
-                rcopy(
-                    here, cr.at[k - 1, q, jj], snd.at[15], c2r.at[k - 1, q, jj], neighbour(q)
-                ).start()
-
-    def deliver():
-        for jj in range(cd):
-            for q in range(4):
-                h, j = q // 2, (q % 2) * cd + jj
-                here = cr.at[n - 2, q, jj]
-                drain(here, c2r.at[n - 2, q, jj])
-                total = out[0, q, jj].astype(F32) + here[...].astype(F32)
-                if h == 0:
-                    zz, yy, at = z, 2 * j + z % 2, y * NX + x
-                else:
-                    zz, yy, at = 2 * j + (1 - y % 2), y, z * NX + x
-                for xd in (0, 1):
-                    piece = fs.at[h, j, xd]
-                    piece[...] = total[8 * xd : 8 * xd + 8].astype(BF)
-                    itself = jnp.logical_and(jnp.logical_and(h_me == h, j_me == j), x == xd)
-
-                    @pl.when(itself)
-                    def _():
-                        cf[at] = piece[...]
-
-                    @pl.when(jnp.logical_not(itself))
-                    def _():
-                        rcopy(
-                            piece, cf.at[at], snd.at[16], one.at[6], dev(role, zz, xd, yy, tp)
-                        ).start()
-
+            drain(hb.at[k, w, 0:16], b2r.at[k, w, i - 1])
+        result = jnp.dot(hb[k, w], dn[...], preferred_element_type=F32)
+        out[k, w] = result.astype(BF).reshape(4, 16, ds)
+
+    def sum_step(k, w):
+        for q in range(4):
+            if k == 1:
+                here = out.at[k, w, q]
+            else:
+                here = cr.at[k - 2, w, q]
+                drain(here, c2r.at[k - 2, w, q])
+                here[...] = (here[...].astype(F32) + out[k, w, q].astype(F32)).astype(BF)
+            rcopy(
+                here, cr.at[k - 1, w, q], snd.at[15], c2r.at[k - 1, w, q], neighbour(q)
+            ).start()
+
+    def deliver(w):
+        for q in range(4):
+            h, e = q // 2, 2 * w + q % 2
+            here = cr.at[n - 2, w, q]
+            drain(here, c2r.at[n - 2, w, q])
+            total = out[0, w, q].astype(F32) + here[...].astype(F32)
+            if h == 0:
+                zz, yy, at = z, (y // 2 - e + ch) % ch * 2 + z % 2, y * NX + x
+            else:
+                zz, yy, at = (z // 2 - e + ch) % ch * 2 + 1 - y % 2, y, z * NX + x
+            for xd in (0, 1):
+                piece = fs.at[w, q, xd]
+                piece[...] = total[8 * xd : 8 * xd + 8].astype(BF)
+
+                def send():
+                    rcopy(piece, cf.at[at], snd.at[16], one.at[6], dev(role, zz, xd, yy, tp)).start()
+
+                if e:
+                    send()
+                    continue
+                itself = jnp.logical_and(h_me == h, x == xd)
+                pl.when(jnp.logical_not(itself))(send)
+
+                @pl.when(itself)
+                def _():
+                    cf[at] = piece[...]
+
+    latent_send()
     gather_start()
-    latent_send()
-    gather_step(0)
-    project_step(0)
-    latent_swap()
-    for k in range(1, n):
-        gather_step(k)
-        project_step(k)
-        hidden_step(k - 1)
-        if k >= 2:
-            down_step(k - 2)
-        if k >= 3:
-            sum_step(k - 2)
-        if k == 1:
+    for u in range(2 * n + 4):
+        if u < 2 * n:
+            gather_step(u // 2, u % 2)
+            project_step(u // 2, u % 2)
+        if 0 <= u - 2 < 2 * n:
+            hidden_step((u - 2) // 2, (u - 2) % 2)
+        if u >= 4:
+            down_step((u - 4) // 2, (u - 4) % 2)
+        if u >= 6:
+            sum_step((u - 4) // 2, (u - 4) % 2)
+        if u == 4:
+            latent_swap()
+        if u == 7:
             latent_project()
-        if k == 3:
+        if u == 10:
             latent_sum()
-        if k == 4:
+        if u == 13:
             handoff_send()
-        if k == 6:
+        if u == 16:
             handoff_share()
-    hidden_step(n - 1)
-    down_step(n - 2)
-    sum_step(n - 2)
-    down_step(n - 1)
-    sum_step(n - 1)
+    deliver(0)
+    deliver(1)
     load_q.wait()
     load_cache.wait()
     make_keys()
     for b in range(8):
         attend(b)
-    deliver()
     drain(cf.at[0 : 2 * n - 1], one.at[6])
     moe_out[...] = jnp.sum(cf[...].astype(F32), axis=0).astype(BF)
 
@@ -428,15 +419,12 @@
     drain(xg.at[0 : n - 1, 0, 0], snd.at[11])
     drain(xg.at[0 : n - 1], snd.at[12])
     drain(pr, snd.at[13])
-    drain(hb.at[:, 0 : 3 * quarter], snd.at[14])
+    drain(hb.at[:, :, 0:48], snd.at[14])
     drain(cr, snd.at[15])
     drain(cf.at[0 : 2 * n - 1], snd.at[16])
 
 
 def fused(n, tok, gain, ids, wts, part, kvg, lens, kvw, gu, dn, queries, cache):
-    ch = n // 2
-    cd = ch // 2
-    step_rows = 4 * cd * 16
     _, ds, f2 = gu.shape
     dsx = ds + 128
     fe, kc = kvw.shape
@@ -453,20 +441,20 @@
         pltpu.VMEM((8, cache.shape[1] + 16, width), BF),
         pltpu.VMEM((8, dsx), BF),
         pltpu.VMEM((2, 8, dsx), BF),
-        pltpu.VMEM((n, 4, cd, 16, dsx), BF),
-        pltpu.VMEM((n, step_rows, f2), F32),
-        pltpu.VMEM((n, step_rows, f2), BF),
-        pltpu.VMEM((n, 3, step_rows // 4, f2), BF),
-        pltpu.VMEM((n, step_rows, f2 // 2), BF),
-        pltpu.VMEM((n, 4, cd, 16, ds), BF),
-        pltpu.VMEM((n - 1, 4, cd, 16, ds), BF),
-        pltpu.VMEM((2, ch, 2, 8, ds), BF),
+        pltpu.VMEM((n, 2, 4, 16, dsx), BF),
+        pltpu.VMEM((n, 2, 64, f2), F32),
+        pltpu.VMEM((n, 2, 64, f2), BF),
+        pltpu.VMEM((n, 2, 3, 16, f2), BF),
+        pltpu.VMEM((n, 2, 64, f2 // 2), BF),
+        pltpu.VMEM((n, 2, 4, 16, ds), BF),
+        pltpu.VMEM((n - 1, 2, 4, 16, ds), BF),
+        pltpu.VMEM((2, 4, 2, 8, ds), BF),
         pltpu.VMEM((2 * n, 8, ds), BF),
         pltpu.VMEM((na, 8, n * fe), BF),
         pltpu.VMEM((na, 8, n * fe), BF),
         pltpu.VMEM((2, n, fe, kc), BF),
-        pltpu.VMEM((na, 8, 2 * kc), F32),
-        pltpu.VMEM((na, 8, 2 * kc), F32),
+        pltpu.VMEM((na, 8, 2 * kc), BF),
+        pltpu.VMEM((na, 8, 2 * kc), BF),
         pltpu.VMEM((2, 8, 2 * kc), BF),
         pltpu.VMEM((n, 8, 2 * kc), BF),
         pltpu.VMEM((na, 8, 2 * kc), BF),
@@ -474,16 +462,17 @@
         pltpu.VMEM((2, 8, 2 * kc), BF),
         pltpu.VMEM((16, width), BF),
         dma((2,)),
-        dma((4, cd)),
-        dma((n, 4, cd)),
-        dma((n, 3)),
-        dma((n, 3)),
-        dma((n - 1, 4, cd)),
+        dma((2, 4)),
+        dma((n, 2, 4)),
+        dma((n, 2, 3)),
+        dma((n, 2, 3)),
+        dma((n - 1, 2, 4)),
         dma((2,)),
         dma((2,)),
         dma((7,)),
         dma((17,)),
         dma((4,)),
+        dma((2, n // 2 + 1)),
     ]
     return pl.pallas_call(
         functools.partial(fused_kernel, n),

time: 96.3 us -> 93.5 us (0.971)
  the two profiles are of different devices: /device:TPU:17 before, /device:TPU:10 now
where the time goes in v3:
time: 93.5 us; the launch traced here: 93.3 us
  Pallas kernels  89.6 us (96%)
  local copies, waits for them, and re-layouts  3.03 us (3%)
    pallas_call x1, Pallas kernels, fused(): pl.pallas_call(functools.partial(fused_kernel, n), out_shape=(jax.ShapeDt...  89.6 us
    unnamed x2, local copies, waits for them, and re-layouts  3.03 us

profile of v3, /device:TPU:10, one launch (start us, length us, event | category | flops | bytes accessed | tf_op | source)
XLA Modules:
  0.0 93.3 jit_solution(8867748721294634392)
XLA Ops:
  0.6 89.6 %shard_map.131 = (bf16[8,32,512]{2,1,0:T(8,128)(2,1)}, bf16[8,1792]{1,0:T(8,128)(2,1)}) custom-call(bf16[1,8,7168]{2,1,0:T(8,128)(2,1)} %tok.1, f32[1,7168]{1,0:T(1,128)} %bitcast.3, s32[8,8]{1,0:T(8,128)} %ids.1, f32[8,8]{1,0:T(8,128)} %wts.1, s32[1,128]{1,0:T(1,128)} %bitcast.5, f32[1,512]{1,0:T(1,128)} %bitcast.4, s32[8]{0:T(128)} %lens.1, ...), custom_call_target="tpu_custom_call" | custom-call | tf_op jit(solution)/shard_map/pallas_call | solution.py:477
  90.3 1.7 %copy.16 = bf16[8,32,512]{2,1,0:T(8,128)(2,1)} copy(bf16[8,32,512]{2,1,0:T(8,128)(2,1)} %get-tuple-element.4) | data formatting | bytes 524288
  91.9 1.4 %copy.17 = bf16[8,1792]{1,0:T(8,128)(2,1)} copy(bf16[8,1792]{1,0:T(8,128)(2,1)} %get-tuple-element.5) | data formatting | bytes 57344
